TPU v7x, 256 devices: a whole 4x4x8 slice. The times are simulated.
256 devices in a mesh: dp: 32 (over z_lo, x, core), tile: 8 (over z_hi, y).
Axes of the slice: x: 4, y: 4, z: 8 (z_hi: 2, z_lo: 4; z = z_hi * 4 + z_lo), core: 2. Of those that a mesh axis runs over, the one named last changes fastest.
Arguments:
- features: bfloat16 [32, 40960, 256], P('dp', 'tile'), may hold values from -6 to 6
- kernels: bfloat16 [32, 100, 256], P('dp'), may hold values from -0.375 to 0.375
- cotangent: bfloat16 [32, 100, 40960], P('dp', None, 'tile'), may hold values from -6 to 6
- w_feat_gate: bfloat16 [256, 256], replicated, may hold values from -0.375 to 0.375
- w_value: bfloat16 [256, 256], replicated, may hold values from -0.375 to 0.375
- w_up: bfloat16 [256, 2048], replicated, may hold values from -0.375 to 0.375
- w_down: bfloat16 [2048, 256], replicated, may hold values from -0.125 to 0.125
Outputs:
- grad_features: float32 [32, 40960, 256], P('dp', 'tile')
- grad_kernels: float32 [32, 100, 256], P('dp')
- grad_feat_gate: float32 [256, 256], replicated
- grad_value: float32 [256, 256], replicated
- grad_up: float32 [256, 2048], replicated
- grad_down: float32 [2048, 256], replicated
All inputs are finite; a program needn't handle non-finite values.
Results may differ from a plain program's by a relative error of at most 0.0034.
Values sent between devices are 32-bit elements; how exact they have to be, the bound alone decides.
A program may use at most 128 MiB of HBM per device.

v0:
```python
import math

import jax
import jax.numpy as jnp
from jax import lax
from jax.sharding import PartitionSpec as P


def normalize(values):
    mean = jnp.mean(values, axis=-1, keepdims=True)
    centred = values - mean
    variance = jnp.mean(centred * centred, axis=-1, keepdims=True)
    return centred * lax.rsqrt(variance + 1e-05)


def head(pooled, kern, w_fg, w_val, w_upper, w_lower):
    top = lax.Precision.HIGHEST
    gate_f = jax.nn.sigmoid(jnp.dot(pooled, w_fg, precision=top))
    value = jnp.dot(pooled, w_val, precision=top)
    first = normalize(gate_f * value + kern)
    hidden = jax.nn.gelu(jnp.dot(first, w_upper, precision=top), approximate=True)
    return normalize(first + jnp.dot(hidden, w_lower, precision=top))


def shards(features, kernels, cotangent, w_feat_gate, w_value, w_up, w_down):
    feat = features[0]
    kern = kernels[0]
    cot = cotangent[0]
    tiles = lax.axis_size("tile")
    scale = 1.0 / math.sqrt(tiles * feat.shape[0])
    weights32 = tuple((w.astype(jnp.float32) for w in (w_feat_gate, w_value, w_up, w_down)))
    logits = jnp.dot(kern, feat.T, preferred_element_type=jnp.float32)
    prob = jax.nn.sigmoid(logits)
    prob_b = prob.astype(jnp.bfloat16)
    pooled = lax.psum(jnp.dot(prob_b, feat, preferred_element_type=jnp.float32), "tile") * scale
    kern32 = kern.astype(jnp.float32)
    partial_new = jnp.dot(cot, feat, preferred_element_type=jnp.float32)
    newk, pull = jax.vjp(head, pooled, kern32, *weights32)
    dnew = lax.psum(partial_new, "tile")
    grads = pull(dnew)
    d_pooled, d_headk = (grads[0], grads[1])
    outs = lax.psum(tuple(grads[2:]), "dp")
    newk_b = newk.astype(jnp.bfloat16)
    d_scaled = (d_pooled * scale).astype(jnp.bfloat16)
    d_prob = jnp.dot(d_scaled, feat.T, preferred_element_type=jnp.float32)
    d_logits = (d_prob * prob * (1.0 - prob)).astype(jnp.bfloat16)
    mask_term = lax.psum(jnp.dot(d_logits, feat, preferred_element_type=jnp.float32), "tile")
    grad_k = d_headk + mask_term
    grad_f = (
        jnp.dot(cot.T, newk_b, preferred_element_type=jnp.float32)
        + jnp.dot(prob_b.T, d_scaled, preferred_element_type=jnp.float32)
        + jnp.dot(d_logits.T, kern, preferred_element_type=jnp.float32)
    )
    return (grad_f[None], grad_k[None], outs[0], outs[1], outs[2], outs[3])


def solution(mesh):
    placed = (P("dp", "tile", None), P("dp", None, None), P("dp", None, "tile"), P(), P(), P(), P())
    return jax.shard_map(
        shards,
        mesh=mesh,
        in_specs=placed,
        out_specs=(P("dp", "tile", None), P("dp", None, None), P(), P(), P(), P()),
        check_vma=False,
    )
```

profile of v0, /device:TPU:1, one launch (start us, length us, event | category | flops | bytes accessed | tf_op | source)
XLA Modules:
  0.0 545.9 jit_solution(5110554213150715773)
XLA Ops:
  7.2 1.7 copy-done
  8.9 1.8 fusion.4
  10.7 1.2 fusion.11
  12.7 1.2 fusion.9
  14.0 103.1 %all-reduce.10.cloned.1.call-done = (f32[100,256]{1,0:T(8,128)}, f32[100,256]{1,0:T(8,128)}) async-done(((f32[100,256]{1,0:T(8,128)}, f32[100,256]{1,0:T(8,128)}), (f32[100,256]{1,0:T(8,128)}, f32[100,256]{1,0:T(8,128)})) %all-reduce.10.cloned.1.call-update) | async-done | bytes 204816 | tf_op jit(solution)/shard_map/psum | solution.py:35
  117.2 1.2 fusion.44
  118.4 1.2 fusion.80
  119.9 1.9 fusion.38
  123.2 1.4 fusion.26
  124.6 1.2 multiply_reduce_fusion
  126.4 1.2 fusion.40
  127.6 3.2 fusion.36
  130.8 3.2 fusion.29
  136.3 1.2 fusion.6
  137.7 1.1 fusion.42
  138.9 2.3 convolution_bitcast_fusion
  142.5 3.2 fusion
  145.7 5.9 %copy.15 = f32[1,5120,256]{2,1,0:T(8,128)} copy(f32[1,5120,256]{1,2,0:T(8,128)} %fusion) | data formatting | bytes 10485760
  151.5 85.0 %all-reduce.6.cloned.1.call-done = f32[100,256]{1,0:T(8,128)} async-done(((f32[100,256]{1,0:T(8,128)}), f32[100,256]{1,0:T(8,128)}) %all-reduce.6.cloned.1.call-update) | async-done | bytes 102416 | tf_op jit(solution)/shard_map/psum | solution.py:47
  238.3 293.2 %all-reduce.8.cloned.1.call-done = (f32[256,256]{1,0:T(8,128)}, f32[256,256]{1,0:T(8,128)}, f32[256,2048]{1,0:T(8,128)}, f32[2048,256]{1,0:T(8,128)}) async-done(((f32[256,256]{1,0:T(8,128)}, f32[256,256]{1,0:T(8,128)}, f32[256,2048]{1,0:T(8,128)}, f32[2048,256]{1,0:T(8,128)}), (f32[256,256]{1,0:T(8,128)}, f32[256,256]{1,0:T(8,128)}, f32[256,2048]{1,0:T(8,128)}, ...) | async-done | bytes 4718608 | tf_op jit(solution)/shard_map/psum | solution.py:42
  531.5 1.7 copy.26
  533.1 1.7 copy.27
  534.8 3.3 copy.28
  538.1 1.3 copy.29
  (54 shorter events, 8.4 us)
Async XLA Ops:
  7.2 1.7 copy-start
  7.2 110.0 %all-reduce.10.cloned.1.call-start = ((), (), s32[]{:S(2)}) async-start(), calls=%async_computation.2 | async-start | bytes 425984 | tf_op jit(solution)/shard_map/psum | solution.py:35
  10.7 1.4 copy-start.1
  10.7 2.0 copy-start.6
  12.7 104.4 %copy-start.10 = (bf16[256,256]{1,0:T(8,128)(2,1)S(1)}, bf16[256,256]{1,0:T(8,128)(2,1)}, u32[]{:S(2)}) copy-start(bf16[256,256]{1,0:T(8,128)(2,1)} %param.11) | copy-start | bytes 393220
  12.7 105.6 %copy-start.12 = (bf16[256,256]{1,0:T(8,128)(2,1)S(1)}, bf16[256,256]{1,0:T(8,128)(2,1)}, u32[]{:S(2)}) copy-start(bf16[256,256]{1,0:T(8,128)(2,1)} %param.10) | copy-start | bytes 393220
  12.7 105.6 %copy-start.13 = (bf16[1,100,256]{2,1,0:T(8,128)(2,1)S(1)}, bf16[1,100,256]{2,1,0:T(8,128)(2,1)}, u32[]{:S(2)}) copy-start(bf16[1,100,256]{2,1,0:T(8,128)(2,1)} %param.8) | copy-start | bytes 153604
  14.0 222.6 %all-reduce.6.cloned.1.call-start = ((), (), s32[]{:S(2)}) async-start(), calls=%async_computation | async-start | bytes 212992 | tf_op jit(solution)/shard_map/psum | solution.py:47
  117.2 4.6 copy-start.14
  119.8 2.9 copy-start.11
  123.1 1.4 copy-start.7
  124.6 1.8 copy-start.9
  130.8 3.5 copy-start.2
  135.3 1.0 copy-start.4
  137.5 394.0 %all-reduce.8.cloned.1.call-start = ((), (), s32[]{:S(2)}) async-start(), calls=%async_computation.1 | async-start | bytes 9437184 | tf_op jit(solution)/shard_map/psum | solution.py:42
  138.9 2.4 copy-start.3
  141.2 1.2 copy-start.5
  534.8 3.3 copy-start.8
Sparse Core Ops, SparseCore 0:
  14.1 103.0 all-reduce.9
  137.6 98.8 all-reduce.5
  240.0 291.3 all-reduce.7
where the time goes:
time: 546 us
  waiting for transfers between devices  481 us (88%)
  matrix products  30 us (5%)
  local copies, waits for them, and re-layouts  18.4 us (3%)
  between operations  14 us (3%)
    psum x1, waiting for transfers between devices, shards(): outs = lax.psum(tuple(grads[2:]), 'dp')  293 us
    psum x1, waiting for transfers between devices, shards(): lax.psum(jnp.dot(prob_b, feat, preferred_element_type=jnp.float32), 'tile')  103 us
    psum x1, waiting for transfers between devices, shards(): lax.psum(jnp.dot(d_logits, feat, preferred_element_type=jnp.float32), 'ti...  85 us
    unnamed x36, local copies, waits for them, and re-layouts  18.4 us
  transfers between devices with their start and end apart: 3, of which 3 were waited for; matrix products, arithmetic and copies ran while one was open for 3% of the time, Pallas kernels for 0%

commit v1 on v0

v1 whole, which is shorter than its diff:
```python
import functools
import math

import jax
import jax.numpy as jnp
from jax import lax
from jax.experimental import pallas as pl
from jax.experimental.pallas import tpu as pltpu
from jax.sharding import PartitionSpec as P

MESH = pl.DeviceIdType.MESH
F32, BF16 = jnp.float32, jnp.bfloat16
X, Y, ZL, ZH = 4, 4, 4, 2
ROWS = 112
PART = 56
CHUNK = 1024
PIECE = 40
BLOCK = ZL * PIECE
SLICE = X * BLOCK
NT = (((1,), (1,)), ((), ()))
NN = (((1,), (0,)), ((), ()))
TN = (((0,), (0,)), ((), ()))


def split(v):
    hi = v.astype(BF16)
    return hi, (v - hi.astype(F32)).astype(BF16)


def dot2(stacked, w, dims):
    both = lax.dot_general(stacked, w, dims, preferred_element_type=F32)
    return both[:ROWS] + both[ROWS:]


def stack(v):
    return jnp.concatenate(split(v), axis=0)


def outer3(a, b):
    ah, al = split(a)
    bh, bl = split(b)
    return lax.dot_general(
        jnp.concatenate([ah, ah, al], axis=0),
        jnp.concatenate([bh, bl, bh], axis=0),
        TN,
        preferred_element_type=F32,
    )


def mean(v):
    return jnp.mean(v, axis=-1, keepdims=True)


def norm(v):
    c = v - mean(v)
    r = lax.rsqrt(mean(c * c) + 1e-05)
    return c * r, r


def norm_back(dy, y, r):
    return r * (dy - mean(dy) - y * mean(dy * y))


def place(ref, v):
    for h in range(2):
        for r in range(2):
            ref[2 * h + r] = v[r * PART : (r + 1) * PART, h * 128 : (h + 1) * 128]


def whole(ref):
    return jnp.concatenate(
        [jnp.concatenate([ref[2 * h], ref[2 * h + 1]], axis=0) for h in range(2)], axis=1
    )


class Place:
    def __init__(self):
        dp, tile = lax.axis_index("dp"), lax.axis_index("tile")
        self.tile = tile
        self.c = lax.rem(dp, 2)
        self.x = lax.rem(dp // 2, X)
        self.zl = dp // (2 * X)
        self.y = lax.rem(tile, Y)
        self.zh = tile // Y

    def at(self, dx=0, dy=0, dzl=0, dzh=0, dc=0):
        x = lax.rem(self.x + dx, X)
        y = lax.rem(self.y + dy, Y)
        zl = lax.rem(self.zl + dzl, ZL)
        zh = lax.rem(self.zh + dzh, ZH)
        c = lax.rem(self.c + dc, 2)
        return ((zl * X + x) * 2 + c, zh * Y + y)


class Sems:
    def __init__(self, send, recv):
        self.send, self.recv, self.n = send, recv, 0

    def copy(self, src, dst, device):
        i = self.n
        self.n += 1
        return pltpu.make_async_remote_copy(
            src_ref=src,
            dst_ref=dst,
            send_sem=self.send.at[i],
            recv_sem=self.recv.at[i],
            device_id=device,
            device_id_type=MESH,
        )


class TileSum:
    def __init__(self, me, sems, mine, got, pair, total):
        self.me, self.sems = me, sems
        self.mine, self.got, self.pair, self.total = mine, got, pair, total
        self.all = []

    def start(self, copies):
        for c in copies:
            c.start()
        self.all += copies
        return copies

    def scatter(self):
        me = self.me
        self.a = self.start(
            [
                self.sems.copy(self.mine.at[lax.rem(me.y + d, Y)], self.got.at[d - 1], me.at(dy=d))
                for d in (1, 2, 3)
            ]
        )

    def exchange(self):
        for c in self.a:
            c.wait_recv()
        me = self.me
        self.pair[0] = (self.mine[me.y] + self.got[0]) + (self.got[1] + self.got[2])
        self.b = self.start([self.sems.copy(self.pair.at[0], self.pair.at[1], me.at(dzh=1))])

    def gather(self):
        self.b[0].wait_recv()
        me = self.me
        self.total[me.y] = self.pair[0] + self.pair[1]
        here = self.total.at[me.y]
        self.d = self.start([self.sems.copy(here, here, me.at(dy=d)) for d in (1, 2, 3)])

    def result(self):
        for c in self.d:
            c.wait_recv()
        return whole(self.total)

    def close(self):
        for c in self.all:
            c.wait_send()


def section(
    scale,
    feat_in,
    kern_in,
    cot_in,
    wfg_in,
    wval_in,
    wup_in,
    wdown_in,
    gathered,
    prob_out,
    dlog_out,
    newk_out,
    dscaled_out,
    gk_out,
    feat,
    cot,
    prob,
    prob_b,
    dlog,
    wfg,
    wval,
    wup,
    wdown,
    acc,
    hid,
    slope,
    dhid,
    tmp,
    sums,
    got,
    pair,
    total,
    terms,
    r0,
    mine,
    r1,
    half,
    r2,
    local,
    send,
    recv,
):
    me = Place()
    sems = Sems(send, recv)
    n = kern_in.shape[0]
    cells = feat_in.shape[0]
    chunks = cells // CHUNK
    ff = wup_in.shape[1] // 256
    c, x, y, zl, zh = me.c, me.x, me.y, me.zl, me.zh

    def part(i):
        return pl.ds(pl.multiple_of(i * CHUNK, CHUNK), CHUNK)

    def feat_copy(i):
        return pltpu.make_async_copy(feat_in.at[part(i), :], feat.at[part(i), :], local.at[i])

    def cot_copy(i):
        return pltpu.make_async_copy(cot_in.at[:, part(i)], cot.at[:, part(i)], local.at[chunks + i])

    for i in range(chunks):
        feat_copy(i).start()
    for i in range(chunks):
        cot_copy(i).start()
    base = 2 * chunks
    weights = [
        pltpu.make_async_copy(a, b, local.at[base + i])
        for i, (a, b) in enumerate(((wfg_in, wfg), (wval_in, wval), (wup_in, wup), (wdown_in, wdown)))
    ]
    for w in weights:
        w.start()
    base += 4

    partners = [me.at(dc=1)]
    partners += [me.at(dy=d) for d in (1, 2, 3)]
    partners += [me.at(dx=d) for d in (1, 2, 3)]
    partners += [me.at(dzl=d % ZL, dzh=d // ZL) for d in range(1, ZL * ZH)]
    barrier = pltpu.get_barrier_semaphore()
    for p in partners:
        pl.semaphore_signal(barrier, inc=1, device_id=p, device_id_type=MESH)

    kern = kern_in[...]

    acc[...] = jnp.zeros_like(acc)

    def pool(i, carry):
        feat_copy(i).wait()
        f = feat[part(i), :]
        p = jax.nn.sigmoid(lax.dot_general(kern, f, NT, preferred_element_type=F32))
        prob[:, part(i)] = p
        pb = p.astype(BF16)
        prob_b[:, part(i)] = pb
        acc[:n, :] += jnp.dot(pb, f, preferred_element_type=F32)
        return carry

    lax.fori_loop(0, chunks, pool, 0)
    sum_p = TileSum(me, sems, sums.at[0], got.at[0], pair.at[0], total.at[0])
    sum_d = TileSum(me, sems, sums.at[1], got.at[1], pair.at[1], total.at[1])
    sum_m = TileSum(me, sems, sums.at[2], got.at[2], pair.at[2], total.at[2])
    place(sums.at[0], acc[...])
    pl.semaphore_wait(barrier, len(partners))
    sum_p.scatter()

    prob_copy = pltpu.make_async_copy(prob_b, prob_out, local.at[base])
    prob_copy.start()

    acc[...] = jnp.zeros_like(acc)

    def new(i, carry):
        cot_copy(i).wait()
        acc[:n, :] += jnp.dot(cot[:, part(i)], feat[part(i), :], preferred_element_type=F32)
        return carry

    lax.fori_loop(0, chunks, new, 0)
    place(sums.at[1], acc[...])
    sum_d.scatter()
    sum_p.exchange()
    sum_d.exchange()
    for w in weights:
        w.wait()
    acc[...] = jnp.zeros_like(acc)
    acc[:n, :] = kern.astype(F32)
    kern32 = acc[...]
    sum_p.gather()
    sum_d.gather()

    pooled = sum_p.result() * scale
    pooled2 = stack(pooled)
    gate = jax.nn.sigmoid(dot2(pooled2, wfg[...], NN))
    value = dot2(pooled2, wval[...], NN)
    k1, rs1 = norm(gate * value + kern32)
    k1s = stack(k1)
    z = k1
    for j in range(ff):
        a = dot2(k1s, wup[:, j * 256 : (j + 1) * 256], NN)
        t = jnp.tanh(0.7978845608028654 * (a + 0.044715 * (a * a * a)))
        up = 0.5 * (1.0 + t)
        h = a * up
        hid[j] = h
        slope[j] = up + 0.5 * a * (1.0 - t * t) * (0.7978845608028654 * (1.0 + 0.134145 * (a * a)))
        z = z + dot2(stack(h), wdown[j * 256 : (j + 1) * 256, :], NN)
    k3, rs3 = norm(z)
    newk_out[...] = k3.astype(BF16)

    dz = norm_back(sum_d.result(), k3, rs3)
    dzs = stack(dz)
    dk1 = dz
    for j in range(ff):
        da = dot2(dzs, wdown[j * 256 : (j + 1) * 256, :], NT) * slope[j]
        dhid[j] = da
        dk1 = dk1 + dot2(stack(da), wup[:, j * 256 : (j + 1) * 256], NT)
    du = norm_back(dk1, k1, rs1)
    dgate = du * value * (gate * (1.0 - gate))
    dvalue = du * gate
    dpooled = dot2(stack(dgate), wfg[...], NT) + dot2(stack(dvalue), wval[...], NT)
    dscaled = (dpooled * scale).astype(BF16)
    dscaled_out[...] = dscaled
    acc[...] = du

    up_term = outer3(k1, dhid[me.tile])
    down_term = outer3(hid[me.tile], dz)
    tmp[0] = outer3(pooled, dgate)
    tmp[1] = outer3(pooled, dvalue)
    own = pl.ds(pl.multiple_of(me.tile * 32, 32), 32)
    for h in range(2):
        lanes = slice(h * 128, (h + 1) * 128)
        terms[h, :256, :] = up_term[:, lanes]
        terms[h, 256:512, :] = down_term[:, lanes]
        terms[h, 512:544, :] = tmp[0, own, lanes]
        terms[h, 544:576, :] = tmp[1, own, lanes]
        terms[h, 576:, :] = jnp.zeros((SLICE - 576, 128), F32)
    c0 = sems.copy(terms.at[1 - c], r0, me.at(dc=1))
    c0.start()

    ds = dscaled[:n]
    sums[2] = jnp.zeros_like(sums[2])

    def mask(i, carry):
        f = feat[part(i), :]
        p = prob[:, part(i)]
        dp = lax.dot_general(ds, f, NT, preferred_element_type=F32)
        dl = (dp * p * (1.0 - p)).astype(BF16)
        dlog[:, part(i)] = dl
        return carry + jnp.dot(dl, f, preferred_element_type=F32)

    macc = lax.fori_loop(0, 2, mask, jnp.zeros((n, 256), F32))
    c0.wait_recv()
    mine[...] = terms[c] + r0[...]

    def rows(i, size):
        return pl.ds(pl.multiple_of(i * size, size), size)

    c1 = [
        sems.copy(mine.at[rows(lax.rem(x + d, X), BLOCK), :], r1.at[d - 1], me.at(dx=d)) for d in (1, 2, 3)
    ]
    for cp in c1:
        cp.start()
    macc = lax.fori_loop(2, chunks, mask, macc)
    dlog_copy = pltpu.make_async_copy(dlog, dlog_out, local.at[base + 1])
    dlog_copy.start()
    gk_out[...] = jnp.zeros_like(gk_out)
    gk_out[:n, :] = macc
    place(sums.at[2], gk_out[...])
    sum_m.scatter()
    for cp in c1:
        cp.wait_recv()
    half[...] = (mine[rows(x, BLOCK), :] + r1[0]) + (r1[1] + r1[2])
    c2 = [
        sems.copy(half.at[rows(lax.rem(zl + d, ZL), PIECE), :], r2.at[d - 1], me.at(dzl=d)) for d in (1, 2, 3)
    ]
    for cp in c2:
        cp.start()
    sum_m.exchange()
    for cp in c2:
        cp.wait_recv()

    spot = rows(x * ZL + zl, PIECE)
    gathered[c, zh, y, spot, :] = (half[rows(zl, PIECE), :] + r2[0]) + (r2[1] + r2[2])
    here = gathered.at[c, zh, y, spot, :]
    cz = [sems.copy(here, here, me.at(dzl=d % ZL, dzh=d // ZL)) for d in range(1, ZL * ZH)]
    for cp in cz:
        cp.start()
    sum_m.gather()
    for cp in cz:
        cp.wait_recv()

    def block(bx, by):
        return gathered.at[c, :, by, rows(bx, BLOCK), :]

    mx, my = 1 - c, c
    started = []

    def send_to(b, **where):
        cp = sems.copy(b, b, me.at(**where))
        cp.start()
        started.append(cp)
        return cp

    first = block(x, y)
    mid = [send_to(first, dx=mx * d, dy=my * d) for d in (1, 3, 2)]
    last = [[send_to(first, dx=my * d, dy=mx * d) for d in (1, 3, 2)]]
    twin = [send_to(first, dc=1)]
    for d, cp in zip((1, 3, 2), mid):
        cp.wait_recv()
        b = block(lax.rem(x + mx * (4 - d), X), lax.rem(y + my * (4 - d), Y))
        last.append([send_to(b, dx=my * e, dy=mx * e) for e in (1, 3, 2)])
        twin.append(send_to(b, dc=1))
    gk_out[...] = sum_m.result() + acc[...]
    for d, group in zip((0, 1, 3, 2), last):
        for e, cp in zip((1, 3, 2), group):
            cp.wait_recv()
            bx = lax.rem(x + mx * (4 - d) + my * (4 - e), X)
            by = lax.rem(y + my * (4 - d) + mx * (4 - e), Y)
            twin.append(send_to(block(bx, by), dc=1))
    for cp in twin:
        cp.wait_recv()

    for s in (sum_p, sum_d, sum_m):
        s.close()
    for cp in [c0] + c1 + c2 + cz + started:
        cp.wait_send()
    prob_copy.wait()
    dlog_copy.wait()


def finish(
    gathered, cot, prob_b, dlog, newk, dscaled, kern, grad_f, g_gate, g_value, g_up, g_down, sem
):
    n = kern.shape[0]
    copies = []
    for h in range(2):
        lanes = pl.ds(h * 128, 128)
        for t in range(ZH * Y):
            src = gathered.at[h, t // Y, t % Y]
            pairs = (
                (src.at[0:256, :], g_up.at[:, pl.ds(t * 256 + h * 128, 128)]),
                (src.at[256:512, :], g_down.at[pl.ds(t * 256, 256), lanes]),
                (src.at[512:544, :], g_gate.at[pl.ds(t * 32, 32), lanes]),
                (src.at[544:576, :], g_value.at[pl.ds(t * 32, 32), lanes]),
            )
            for a, b in pairs:
                copies.append(pltpu.make_async_copy(a, b, sem.at[len(copies)]))

    @pl.when(pl.program_id(0) == 0)
    def _():
        for cp in copies:
            cp.start()

    def term(a, b):
        return lax.dot_general(a, b, TN, preferred_element_type=F32)

    grad_f[...] = term(cot[...], newk[:n, :]) + term(prob_b[...], dscaled[:n, :]) + term(dlog[...], kern[...])

    @pl.when(pl.program_id(0) == pl.num_programs(0) - 1)
    def _():
        for cp in copies:
            cp.wait()


def shards(features, kernels, cotangent, w_feat_gate, w_value, w_up, w_down):
    feat, kern, cot = features[0], kernels[0], cotangent[0]
    n, channels = kern.shape
    cells = feat.shape[0]
    chunks = cells // CHUNK
    ff = w_up.shape[1] // 256
    scale = 1.0 / math.sqrt(lax.axis_size("tile") * cells)
    anywhere = pl.BlockSpec(memory_space=pl.ANY)
    vmem = pl.BlockSpec(memory_space=pltpu.VMEM)
    copies = 64
    shape = jax.ShapeDtypeStruct
    gathered, prob_b, dlog, newk, dscaled, gk = pl.pallas_call(
        functools.partial(section, scale),
        out_shape=(
            shape((2, ZH, Y, SLICE, 128), F32),
            shape((n, cells), BF16),
            shape((n, cells), BF16),
            shape((ROWS, channels), BF16),
            shape((ROWS, channels), BF16),
            shape((ROWS, channels), F32),
        ),
        in_specs=[anywhere, vmem, anywhere, anywhere, anywhere, anywhere, anywhere],
        out_specs=(vmem, anywhere, anywhere, vmem, vmem, vmem),
        scratch_shapes=[
            pltpu.VMEM((cells, channels), BF16),
            pltpu.VMEM((n, cells), BF16),
            pltpu.VMEM((n, cells), F32),
            pltpu.VMEM((n, cells), BF16),
            pltpu.VMEM((n, cells), BF16),
            pltpu.VMEM(w_feat_gate.shape, BF16),
            pltpu.VMEM(w_value.shape, BF16),
            pltpu.VMEM(w_up.shape, BF16),
            pltpu.VMEM(w_down.shape, BF16),
            pltpu.VMEM((ROWS, channels), F32),
            pltpu.VMEM((ff, ROWS, 256), F32),
            pltpu.VMEM((ff, ROWS, 256), F32),
            pltpu.VMEM((ff, ROWS, 256), F32),
            pltpu.VMEM((2, 256, 256), F32),
            pltpu.VMEM((3, 4, PART, 128), F32),
            pltpu.VMEM((3, 3, PART, 128), F32),
            pltpu.VMEM((3, 2, PART, 128), F32),
            pltpu.VMEM((3, 4, PART, 128), F32),
            pltpu.VMEM((2, SLICE, 128), F32),
            pltpu.VMEM((SLICE, 128), F32),
            pltpu.VMEM((SLICE, 128), F32),
            pltpu.VMEM((3, BLOCK, 128), F32),
            pltpu.VMEM((BLOCK, 128), F32),
            pltpu.VMEM((3, PIECE, 128), F32),
            pltpu.SemaphoreType.DMA((2 * chunks + 6,)),
            pltpu.SemaphoreType.DMA((copies + 8,)),
            pltpu.SemaphoreType.DMA((copies + 8,)),
        ],
        compiler_params=pltpu.CompilerParams(
            collective_id=0, has_side_effects=True, vmem_limit_bytes=40 * 2**20
        ),
        name="section",
    )(feat, kern, cot, w_feat_gate, w_value, w_up, w_down)

    wide = pl.BlockSpec((n, CHUNK), lambda i: (0, i))
    grad_f, g_gate, g_value, g_up, g_down = pl.pallas_call(
        finish,
        grid=(chunks,),
        out_shape=(
            shape((cells, channels), F32),
            shape(w_feat_gate.shape, F32),
            shape(w_value.shape, F32),
            shape(w_up.shape, F32),
            shape(w_down.shape, F32),
        ),
        in_specs=[anywhere, wide, wide, wide, vmem, vmem, vmem],
        out_specs=(
            pl.BlockSpec((CHUNK, channels), lambda i: (i, 0)),
            anywhere,
            anywhere,
            anywhere,
            anywhere,
        ),
        scratch_shapes=[pltpu.SemaphoreType.DMA((ZH * Y * 2 * 4,))],
        compiler_params=pltpu.CompilerParams(vmem_limit_bytes=24 * 2**20),
        name="finish",
    )(gathered, cot, prob_b, dlog, newk, dscaled, kern)
    return (grad_f[None], gk[None, :n], g_gate, g_value, g_up, g_down)


def solution(mesh):
    placed = (P("dp", "tile", None), P("dp", None, None), P("dp", None, "tile"), P(), P(), P(), P())
    return jax.shard_map(
        shards,
        mesh=mesh,
        in_specs=placed,
        out_specs=(P("dp", "tile", None), P("dp", None, None), P(), P(), P(), P()),
        check_vma=False,
    )
```

time: 546 us -> 86.2 us (0.16)
  waiting for transfers between devices: 481 us -> 0 us
  Pallas kernels: 0 us -> 76.4 us
  matrix products: 30 us -> 0 us
  between operations: 14 us -> 0.67 us
  local copies, waits for them, and re-layouts: 18.4 us -> 8.78 us
    psum x3 -> x0, waiting for transfers between devices: 481 us -> none  [the longest x1 293 us: shards(): outs = lax.psum(tuple(grads[2:]), 'dp')]
    pallas_call x0 -> x2, Pallas kernels: none -> 76.4 us  [the longest x1 69.8 us: shards(): pl.pallas_call(functools.partial(section, scale), out_shape=(shape((2, ZH...]
    dot_general x20 -> x0, matrix products: 30 us -> none  [the longest x3 6.35 us: head(): jnp.dot(first, w_upper, precision=top)]
    unnamed x36 -> x15, local copies, waits for them, and re-layouts: 18.4 us -> 8.78 us
  transfers between devices with their start and end apart: 3 -> 0, of which waited for: 3 -> 0; matrix products, arithmetic and copies ran while one was open for 3% -> 0% of each run, Pallas kernels for 0% -> 0%
where the time goes in v1:
time: 86.2 us; the launch traced here: 85.9 us
  Pallas kernels  76.4 us (89%)
  local copies, waits for them, and re-layouts  8.78 us (10%)
    pallas_call x1, Pallas kernels, shards(): pl.pallas_call(functools.partial(section, scale), out_shape=(shape((2, ZH...  69.8 us
    unnamed x15, local copies, waits for them, and re-layouts  8.78 us
    pallas_call x1, Pallas kernels, shards(): pl.pallas_call(finish, grid=(chunks,), out_shape=(shape((cells, channels)...  6.59 us

profile of v1, /device:TPU:1, one launch (start us, length us, event | category | flops | bytes accessed | tf_op | source)
XLA Modules:
  0.0 85.9 jit_solution(6312458643188468568)
XLA Ops:
  0.6 0.0 copy-start
  0.6 1.2 %copy-done = bf16[1,100,5120]{2,1,0:T(8,128)(2,1)S(1)} copy-done((bf16[1,100,5120]{2,1,0:T(8,128)(2,1)S(1)}, bf16[1,100,5120]{2,1,0:T(8,128)(2,1)}, u32[]{:S(2)}) %copy-start) | copy-done | bytes 1024024
  1.9 0.0 copy-start.1
  1.9 1.7 %copy-done.1 = bf16[1,5120,256]{2,1,0:T(8,128)(2,1)S(1)} copy-done((bf16[1,5120,256]{2,1,0:T(8,128)(2,1)S(1)}, bf16[1,5120,256]{2,1,0:T(8,128)(2,1)}, u32[]{:S(2)}) %copy-start.1) | copy-done | bytes 2621464
  3.6 0.0 copy-start.2
  3.6 1.2 %copy-done.2 = bf16[256,2048]{1,0:T(8,128)(2,1)S(1)} copy-done((bf16[256,2048]{1,0:T(8,128)(2,1)S(1)}, bf16[256,2048]{1,0:T(8,128)(2,1)}, u32[]{:S(2)}) %copy-start.2) | copy-done | bytes 1048600
  4.8 0.0 copy-start.3
  4.8 1.2 %copy-done.3 = bf16[2048,256]{1,0:T(8,128)(2,1)S(1)} copy-done((bf16[2048,256]{1,0:T(8,128)(2,1)S(1)}, bf16[2048,256]{1,0:T(8,128)(2,1)}, u32[]{:S(2)}) %copy-start.3) | copy-done | bytes 1048600
  6.1 0.0 copy-start.4
  6.1 0.8 copy-done.4
  6.9 0.0 copy-start.5
  6.9 0.9 %copy-done.5 = bf16[256,256]{1,0:T(8,128)(2,1)S(1)} copy-done((bf16[256,256]{1,0:T(8,128)(2,1)S(1)}, bf16[256,256]{1,0:T(8,128)(2,1)}, u32[]{:S(2)}) %copy-start.5) | copy-done | bytes 131096
  7.8 0.0 copy-start.6
  7.8 0.9 %copy-done.6 = bf16[256,256]{1,0:T(8,128)(2,1)S(1)} copy-done((bf16[256,256]{1,0:T(8,128)(2,1)S(1)}, bf16[256,256]{1,0:T(8,128)(2,1)}, u32[]{:S(2)}) %copy-start.6) | copy-done | bytes 131096
  8.7 69.8 %section.1 = (f32[2,2,4,640,128]{4,3,2,1,0:T(8,128)S(1)}, bf16[100,5120]{1,0:T(8,128)(2,1)S(1)}, bf16[100,5120]{1,0:T(8,128)(2,1)S(1)}, bf16[112,256]{1,0:T(8,12...) custom-call(bf16[5120,256]{1,0:T(8,128)(2,1)S(1)} %bitcast.8, bf16[100,256]{1,0:T(8,128)(2,1)S(1)} %bitcast.9, ...), custom_call_target="tpu_custom_call" | custom-call | tf_op jit(solution)/shard_map/section/pallas_call | solution.py:467
  78.5 0.7 copy.13
  79.3 6.6 %finish.1 = (f32[5120,256]{1,0:T(8,128)}, f32[256,256]{1,0:T(8,128)}, f32[256,256]{1,0:T(8,128)}, f32[256,2048]{1,0:T(8,128)}, f32[2048,256]{1,0:T(8,128)}) custom-call(f32[2,2,4,640,128]{4,3,2,1,0:T(8,128)S(1)} %get-tuple-element.17.gathered, bf16[100,5120]{1,0:T(8,128)(2,1)S(1)} %bitcast.7, bf16[100,5120]{1,0:T(8,128)(2,1)S(1)} %get-tuple-element.18.prob_b, ...), custom_call_target="tpu_custom_call" | custom-call | tf_op jit(solution)/shard_map/finish/pallas_call | solution.py:515
  (1 shorter events, 0.0 us)
Async XLA Ops:
  0.6 1.2 %copy-start = (bf16[1,100,5120]{2,1,0:T(8,128)(2,1)S(1)}, bf16[1,100,5120]{2,1,0:T(8,128)(2,1)}, u32[]{:S(2)}) copy-start(bf16[1,100,5120]{2,1,0:T(8,128)(2,1)} %param.9) | copy-start | bytes 3072004
  1.9 1.7 %copy-start.1 = (bf16[1,5120,256]{2,1,0:T(8,128)(2,1)S(1)}, bf16[1,5120,256]{2,1,0:T(8,128)(2,1)}, u32[]{:S(2)}) copy-start(bf16[1,5120,256]{2,1,0:T(8,128)(2,1)} %param.7) | copy-start | bytes 7864324
  3.6 1.2 %copy-start.2 = (bf16[256,2048]{1,0:T(8,128)(2,1)S(1)}, bf16[256,2048]{1,0:T(8,128)(2,1)}, u32[]{:S(2)}) copy-start(bf16[256,2048]{1,0:T(8,128)(2,1)} %wup_in.1) | copy-start | bytes 3145732
  4.8 1.2 %copy-start.3 = (bf16[2048,256]{1,0:T(8,128)(2,1)S(1)}, bf16[2048,256]{1,0:T(8,128)(2,1)}, u32[]{:S(2)}) copy-start(bf16[2048,256]{1,0:T(8,128)(2,1)} %wdown_in.1) | copy-start | bytes 3145732
  6.1 0.8 copy-start.4
  6.9 0.9 %copy-start.5 = (bf16[256,256]{1,0:T(8,128)(2,1)S(1)}, bf16[256,256]{1,0:T(8,128)(2,1)}, u32[]{:S(2)}) copy-start(bf16[256,256]{1,0:T(8,128)(2,1)} %wfg_in.1) | copy-start | bytes 393220
  7.8 0.9 %copy-start.6 = (bf16[256,256]{1,0:T(8,128)(2,1)S(1)}, bf16[256,256]{1,0:T(8,128)(2,1)}, u32[]{:S(2)}) copy-start(bf16[256,256]{1,0:T(8,128)(2,1)} %wval_in.1) | copy-start | bytes 393220

commit v2 on v1

--- a/solution.py
+++ b/solution.py
@@ -14,9 +14,9 @@
 ROWS = 112
 PART = 56
 CHUNK = 1024
-PIECE = 40
-BLOCK = ZL * PIECE
-SLICE = X * BLOCK
+PIECE = 32
+SMALL = 16
+BLOCK = ZL * PIECE + SMALL
 NT = (((1,), (1,)), ((), ()))
 NN = (((1,), (0,)), ((), ()))
 TN = (((0,), (0,)), ((), ()))
@@ -164,13 +164,11 @@
     wup_in,
     wdown_in,
     gathered,
-    prob_out,
-    dlog_out,
-    newk_out,
-    dscaled_out,
+    gf_out,
     gk_out,
     feat,
     cot,
+    kern_v,
     prob,
     prob_b,
     dlog,
@@ -179,6 +177,7 @@
     wup,
     wdown,
     acc,
+    acc2,
     hid,
     slope,
     dhid,
@@ -193,6 +192,7 @@
     r1,
     half,
     r2,
+    small,
     local,
     send,
     recv,
@@ -214,6 +214,8 @@
     def cot_copy(i):
         return pltpu.make_async_copy(cot_in.at[:, part(i)], cot.at[:, part(i)], local.at[chunks + i])
 
+    kern_copy = pltpu.make_async_copy(kern_in, kern_v, local.at[2 * chunks + 4])
+    kern_copy.start()
     for i in range(chunks):
         feat_copy(i).start()
     for i in range(chunks):
@@ -225,7 +227,6 @@
     ]
     for w in weights:
         w.start()
-    base += 4
 
     partners = [me.at(dc=1)]
     partners += [me.at(dy=d) for d in (1, 2, 3)]
@@ -235,7 +236,8 @@
     for p in partners:
         pl.semaphore_signal(barrier, inc=1, device_id=p, device_id_type=MESH)
 
-    kern = kern_in[...]
+    kern_copy.wait()
+    kern = kern_v[...]
 
     acc[...] = jnp.zeros_like(acc)
 
@@ -256,9 +258,6 @@
     place(sums.at[0], acc[...])
     pl.semaphore_wait(barrier, len(partners))
     sum_p.scatter()
-
-    prob_copy = pltpu.make_async_copy(prob_b, prob_out, local.at[base])
-    prob_copy.start()
 
     acc[...] = jnp.zeros_like(acc)
 
@@ -296,7 +295,7 @@
         slope[j] = up + 0.5 * a * (1.0 - t * t) * (0.7978845608028654 * (1.0 + 0.134145 * (a * a)))
         z = z + dot2(stack(h), wdown[j * 256 : (j + 1) * 256, :], NN)
     k3, rs3 = norm(z)
-    newk_out[...] = k3.astype(BF16)
+    newk = k3.astype(BF16)[:n]
 
     dz = norm_back(sum_d.result(), k3, rs3)
     dzs = stack(dz)
@@ -310,26 +309,24 @@
     dvalue = du * gate
     dpooled = dot2(stack(dgate), wfg[...], NT) + dot2(stack(dvalue), wval[...], NT)
     dscaled = (dpooled * scale).astype(BF16)
-    dscaled_out[...] = dscaled
     acc[...] = du
 
     up_term = outer3(k1, dhid[me.tile])
     down_term = outer3(hid[me.tile], dz)
     tmp[0] = outer3(pooled, dgate)
     tmp[1] = outer3(pooled, dvalue)
-    own = pl.ds(pl.multiple_of(me.tile * 32, 32), 32)
     for h in range(2):
         lanes = slice(h * 128, (h + 1) * 128)
-        terms[h, :256, :] = up_term[:, lanes]
-        terms[h, 256:512, :] = down_term[:, lanes]
-        terms[h, 512:544, :] = tmp[0, own, lanes]
-        terms[h, 544:576, :] = tmp[1, own, lanes]
-        terms[h, 576:, :] = jnp.zeros((SLICE - 576, 128), F32)
+        for i in range(X):
+            own = pl.ds(pl.multiple_of(me.tile * 32 + i * 8, 8), 8)
+            terms[h, i, :64, :] = up_term[i * 64 : (i + 1) * 64, lanes]
+            terms[h, i, 64:128, :] = down_term[i * 64 : (i + 1) * 64, lanes]
+            terms[h, i, 128:136, :] = tmp[0, own, lanes]
+            terms[h, i, 136:, :] = tmp[1, own, lanes]
     c0 = sems.copy(terms.at[1 - c], r0, me.at(dc=1))
     c0.start()
 
     ds = dscaled[:n]
-    sums[2] = jnp.zeros_like(sums[2])
 
     def mask(i, carry):
         f = feat[part(i), :]
@@ -339,118 +336,169 @@
         dlog[:, part(i)] = dl
         return carry + jnp.dot(dl, f, preferred_element_type=F32)
 
+    def term(a, b):
+        return lax.dot_general(a, b, TN, preferred_element_type=F32)
+
+    def features(i):
+        gf_out[part(i), :] = (
+            term(cot[:, part(i)], newk) + term(prob_b[:, part(i)], ds) + term(dlog[:, part(i)], kern)
+        )
+
     macc = lax.fori_loop(0, 2, mask, jnp.zeros((n, 256), F32))
     c0.wait_recv()
     mine[...] = terms[c] + r0[...]
-
-    def rows(i, size):
-        return pl.ds(pl.multiple_of(i * size, size), size)
-
-    c1 = [
-        sems.copy(mine.at[rows(lax.rem(x + d, X), BLOCK), :], r1.at[d - 1], me.at(dx=d)) for d in (1, 2, 3)
-    ]
+    c1 = [sems.copy(mine.at[lax.rem(x + d, X)], r1.at[d - 1], me.at(dx=d)) for d in (1, 3, 2)]
     for cp in c1:
         cp.start()
     macc = lax.fori_loop(2, chunks, mask, macc)
-    dlog_copy = pltpu.make_async_copy(dlog, dlog_out, local.at[base + 1])
-    dlog_copy.start()
-    gk_out[...] = jnp.zeros_like(gk_out)
-    gk_out[:n, :] = macc
-    place(sums.at[2], gk_out[...])
+    acc2[...] = jnp.zeros_like(acc2)
+    acc2[:n, :] = macc
+    place(sums.at[2], acc2[...])
     sum_m.scatter()
     for cp in c1:
         cp.wait_recv()
-    half[...] = (mine[rows(x, BLOCK), :] + r1[0]) + (r1[1] + r1[2])
-    c2 = [
-        sems.copy(half.at[rows(lax.rem(zl + d, ZL), PIECE), :], r2.at[d - 1], me.at(dzl=d)) for d in (1, 2, 3)
-    ]
+    half[...] = (mine[x] + r1[0]) + (r1[1] + r1[2])
+
+    def piece(i):
+        return pl.ds(pl.multiple_of(i * PIECE, PIECE), PIECE)
+
+    tail = pl.ds(ZL * PIECE, SMALL)
+    small[zl] = half[ZL * PIECE :, :]
+    c2 = []
+    for d in (1, 3, 2):
+        c2.append(sems.copy(half.at[piece(lax.rem(zl + d, ZL)), :], r2.at[d - 1], me.at(dzl=d)))
+        c2.append(sems.copy(half.at[tail, :], small.at[zl], me.at(dzl=d)))
     for cp in c2:
         cp.start()
     sum_m.exchange()
+    features(0)
     for cp in c2:
         cp.wait_recv()
 
-    spot = rows(x * ZL + zl, PIECE)
-    gathered[c, zh, y, spot, :] = (half[rows(zl, PIECE), :] + r2[0]) + (r2[1] + r2[2])
-    here = gathered.at[c, zh, y, spot, :]
-    cz = [sems.copy(here, here, me.at(dzl=d % ZL, dzh=d // ZL)) for d in range(1, ZL * ZH)]
-    for cp in cz:
+    gathered[c, zh, y, x, piece(zl), :] = (half[piece(zl), :] + r2[0]) + (r2[1] + r2[2])
+    gathered[c, zh, y, x, tail, :] = (small[0] + small[1]) + (small[2] + small[3])
+    here = gathered.at[c, zh, y, x, piece(zl), :]
+    here_tail = gathered.at[c, zh, y, x, tail, :]
+    far = [sems.copy(here, here, me.at(dzl=d, dzh=1)) for d in (0, 1, 3, 2)]
+    far.append(sems.copy(here_tail, here_tail, me.at(dzh=1)))
+    near = [sems.copy(here, here, me.at(dzl=d)) for d in (1, 3, 2)]
+    for cp in near + far:
         cp.start()
     sum_m.gather()
-    for cp in cz:
-        cp.wait_recv()
-
-    def block(bx, by):
-        return gathered.at[c, :, by, rows(bx, BLOCK), :]
+    features(1)
 
     mx, my = 1 - c, c
+
+    def block(q, m, l):
+        bx = lax.rem(x + mx * m + my * l, X)
+        by = lax.rem(y + my * m + mx * l, Y)
+        return gathered.at[c, lax.rem(zh + q, ZH), by, bx]
+
     started = []
-
-    def send_to(b, **where):
-        cp = sems.copy(b, b, me.at(**where))
+    twin = []
+
+    def send_to(b, device):
+        cp = sems.copy(b, b, device)
         cp.start()
         started.append(cp)
         return cp
 
-    first = block(x, y)
-    mid = [send_to(first, dx=mx * d, dy=my * d) for d in (1, 3, 2)]
-    last = [[send_to(first, dx=my * d, dy=mx * d) for d in (1, 3, 2)]]
-    twin = [send_to(first, dc=1)]
-    for d, cp in zip((1, 3, 2), mid):
+    def along_mid(d):
+        return me.at(dx=mx * d, dy=my * d)
+
+    def along_last(d):
+        return me.at(dx=my * d, dy=mx * d)
+
+    def to_twin(b):
+        twin.append(send_to(b, me.at(dc=1)))
+
+    mids, lasts, halves = {}, {}, {}
+
+    def open_mid(q):
+        b = block(q, 0, 0)
+        for d in (1, 3, 2):
+            mids[q, d] = send_to(b, along_mid(d))
+
+    def open_last(q, m):
+        if m:
+            mids[q, m].wait_recv()
+        b = block(q, (4 - m) % 4, 0)
+        lasts[q, m] = [send_to(b, along_last(d)) for d in (1, 3)]
+        to_twin(b)
+
+    def relay(q, m):
+        halves[q, m] = []
+        for d, first, cp in zip((1, 3), (0, BLOCK // 2), lasts[q, m]):
+            cp.wait_recv()
+            b = block(q, (4 - m) % 4, 4 - d)
+            halves[q, m].append(send_to(b.at[pl.ds(first, BLOCK // 2), :], along_last(d)))
+            to_twin(b)
+
+    def close(q, m):
+        for cp in halves[q, m]:
+            cp.wait_recv()
+        to_twin(block(q, (4 - m) % 4, 2))
+
+    for cp in near:
         cp.wait_recv()
-        b = block(lax.rem(x + mx * (4 - d), X), lax.rem(y + my * (4 - d), Y))
-        last.append([send_to(b, dx=my * e, dy=mx * e) for e in (1, 3, 2)])
-        twin.append(send_to(b, dc=1))
-    gk_out[...] = sum_m.result() + acc[...]
-    for d, group in zip((0, 1, 3, 2), last):
-        for e, cp in zip((1, 3, 2), group):
-            cp.wait_recv()
-            bx = lax.rem(x + mx * (4 - d) + my * (4 - e), X)
-            by = lax.rem(y + my * (4 - d) + mx * (4 - e), Y)
-            twin.append(send_to(block(bx, by), dc=1))
+    open_mid(0)
+    open_last(0, 0)
+    features(2)
+    for cp in far:
+        cp.wait_recv()
+    open_mid(1)
+    open_last(1, 0)
+    features(3)
+    relay(0, 0)
+    open_last(0, 1)
+    open_last(0, 3)
+    relay(1, 0)
+    open_last(1, 1)
+    open_last(1, 3)
+    open_last(0, 2)
+    open_last(1, 2)
+    close(0, 0)
+    features(4)
+    relay(0, 1)
+    relay(0, 3)
+    close(1, 0)
+    relay(1, 1)
+    relay(1, 3)
+    gk_out[:, 0, :] = (sum_m.result() + acc[...])[:n]
+    close(0, 1)
+    close(0, 3)
+    relay(0, 2)
+    relay(1, 2)
+    close(1, 1)
+    close(1, 3)
+    close(0, 2)
+    close(1, 2)
     for cp in twin:
         cp.wait_recv()
 
     for s in (sum_p, sum_d, sum_m):
         s.close()
-    for cp in [c0] + c1 + c2 + cz + started:
+    for cp in [c0] + c1 + c2 + near + far + started:
         cp.wait_send()
-    prob_copy.wait()
-    dlog_copy.wait()
-
-
-def finish(
-    gathered, cot, prob_b, dlog, newk, dscaled, kern, grad_f, g_gate, g_value, g_up, g_down, sem
-):
-    n = kern.shape[0]
-    copies = []
+
+
+def finish(gathered, gf, gk, grad_f, grad_k, g_gate, g_value, g_up, g_down, sem):
+    pairs = [(gf, grad_f), (gk, grad_k)]
     for h in range(2):
         lanes = pl.ds(h * 128, 128)
         for t in range(ZH * Y):
             src = gathered.at[h, t // Y, t % Y]
-            pairs = (
-                (src.at[0:256, :], g_up.at[:, pl.ds(t * 256 + h * 128, 128)]),
-                (src.at[256:512, :], g_down.at[pl.ds(t * 256, 256), lanes]),
-                (src.at[512:544, :], g_gate.at[pl.ds(t * 32, 32), lanes]),
-                (src.at[544:576, :], g_value.at[pl.ds(t * 32, 32), lanes]),
-            )
-            for a, b in pairs:
-                copies.append(pltpu.make_async_copy(a, b, sem.at[len(copies)]))
-
-    @pl.when(pl.program_id(0) == 0)
-    def _():
-        for cp in copies:
-            cp.start()
-
-    def term(a, b):
-        return lax.dot_general(a, b, TN, preferred_element_type=F32)
-
-    grad_f[...] = term(cot[...], newk[:n, :]) + term(prob_b[...], dscaled[:n, :]) + term(dlog[...], kern[...])
-
-    @pl.when(pl.program_id(0) == pl.num_programs(0) - 1)
-    def _():
-        for cp in copies:
-            cp.wait()
+            pairs += [
+                (src.at[:, 0:64, :], g_up.at[:, :, pl.ds(t * 256 + h * 128, 128)]),
+                (src.at[:, 64:128, :], g_down.at[t, :, :, lanes]),
+                (src.at[:, 128:136, :], g_gate.at[t, :, :, lanes]),
+                (src.at[:, 136:144, :], g_value.at[t, :, :, lanes]),
+            ]
+    copies = [pltpu.make_async_copy(a, b, sem.at[i]) for i, (a, b) in enumerate(pairs)]
+    for cp in copies:
+        cp.start()
+    for cp in copies:
+        cp.wait()
 
 
 def shards(features, kernels, cotangent, w_feat_gate, w_value, w_up, w_down):
@@ -461,24 +509,27 @@
     ff = w_up.shape[1] // 256
     scale = 1.0 / math.sqrt(lax.axis_size("tile") * cells)
     anywhere = pl.BlockSpec(memory_space=pl.ANY)
+
+    def hbm(v):
+        return pltpu.with_memory_space_constraint(v, pltpu.HBM)
+
+    kern, cot = hbm(kern), hbm(cot)
     vmem = pl.BlockSpec(memory_space=pltpu.VMEM)
-    copies = 64
+    copies = 128
     shape = jax.ShapeDtypeStruct
-    gathered, prob_b, dlog, newk, dscaled, gk = pl.pallas_call(
+    gathered, gf, gk = pl.pallas_call(
         functools.partial(section, scale),
         out_shape=(
-            shape((2, ZH, Y, SLICE, 128), F32),
-            shape((n, cells), BF16),
-            shape((n, cells), BF16),
-            shape((ROWS, channels), BF16),
-            shape((ROWS, channels), BF16),
-            shape((ROWS, channels), F32),
+            shape((2, ZH, Y, X, BLOCK, 128), F32),
+            shape((cells, channels), F32),
+            shape((n, 1, channels), F32),
         ),
-        in_specs=[anywhere, vmem, anywhere, anywhere, anywhere, anywhere, anywhere],
-        out_specs=(vmem, anywhere, anywhere, vmem, vmem, vmem),
+        in_specs=[anywhere] * 7,
+        out_specs=(vmem, vmem, vmem),
         scratch_shapes=[
             pltpu.VMEM((cells, channels), BF16),
             pltpu.VMEM((n, cells), BF16),
+            pltpu.VMEM((n, channels), BF16),
             pltpu.VMEM((n, cells), F32),
             pltpu.VMEM((n, cells), BF16),
             pltpu.VMEM((n, cells), BF16),
@@ -486,6 +537,7 @@
             pltpu.VMEM(w_value.shape, BF16),
             pltpu.VMEM(w_up.shape, BF16),
             pltpu.VMEM(w_down.shape, BF16),
+            pltpu.VMEM((ROWS, channels), F32),
             pltpu.VMEM((ROWS, channels), F32),
             pltpu.VMEM((ff, ROWS, 256), F32),
             pltpu.VMEM((ff, ROWS, 256), F32),
@@ -495,46 +547,47 @@
             pltpu.VMEM((3, 3, PART, 128), F32),
             pltpu.VMEM((3, 2, PART, 128), F32),
             pltpu.VMEM((3, 4, PART, 128), F32),
-            pltpu.VMEM((2, SLICE, 128), F32),
-            pltpu.VMEM((SLICE, 128), F32),
-            pltpu.VMEM((SLICE, 128), F32),
+            pltpu.VMEM((2, X, BLOCK, 128), F32),
+            pltpu.VMEM((X, BLOCK, 128), F32),
+            pltpu.VMEM((X, BLOCK, 128), F32),
             pltpu.VMEM((3, BLOCK, 128), F32),
             pltpu.VMEM((BLOCK, 128), F32),
             pltpu.VMEM((3, PIECE, 128), F32),
-            pltpu.SemaphoreType.DMA((2 * chunks + 6,)),
-            pltpu.SemaphoreType.DMA((copies + 8,)),
-            pltpu.SemaphoreType.DMA((copies + 8,)),
+            pltpu.VMEM((ZL, SMALL, 128), F32),
+            pltpu.SemaphoreType.DMA((2 * chunks + 5,)),
+            pltpu.SemaphoreType.DMA((copies,)),
+            pltpu.SemaphoreType.DMA((copies,)),
         ],
         compiler_params=pltpu.CompilerParams(
-            collective_id=0, has_side_effects=True, vmem_limit_bytes=40 * 2**20
+            collective_id=0, has_side_effects=True, vmem_limit_bytes=32 * 2**20
         ),
         name="section",
-    )(feat, kern, cot, w_feat_gate, w_value, w_up, w_down)
-
-    wide = pl.BlockSpec((n, CHUNK), lambda i: (0, i))
-    grad_f, g_gate, g_value, g_up, g_down = pl.pallas_call(
+    )(hbm(feat), kern, cot, hbm(w_feat_gate), hbm(w_value), hbm(w_up), hbm(w_down))
+
+    tiles = ZH * Y
+    grad_f, grad_k, g_gate, g_value, g_up, g_down = pl.pallas_call(
         finish,
-        grid=(chunks,),
         out_shape=(
             shape((cells, channels), F32),
-            shape(w_feat_gate.shape, F32),
-            shape(w_value.shape, F32),
-            shape(w_up.shape, F32),
-            shape(w_down.shape, F32),
+            shape((n, 1, channels), F32),
+            shape((tiles, X, 8, channels), F32),
+            shape((tiles, X, 8, channels), F32),
+            shape((X, 64, w_up.shape[1]), F32),
+            shape((tiles, X, 64, channels), F32),
         ),
-        in_specs=[anywhere, wide, wide, wide, vmem, vmem, vmem],
-        out_specs=(
-            pl.BlockSpec((CHUNK, channels), lambda i: (i, 0)),
-            anywhere,
-            anywhere,
-            anywhere,
-            anywhere,
-        ),
-        scratch_shapes=[pltpu.SemaphoreType.DMA((ZH * Y * 2 * 4,))],
-        compiler_params=pltpu.CompilerParams(vmem_limit_bytes=24 * 2**20),
+        in_specs=[anywhere] * 3,
+        out_specs=(anywhere,) * 6,
+        scratch_shapes=[pltpu.SemaphoreType.DMA((2 + tiles * 2 * 4,))],
         name="finish",
-    )(gathered, cot, prob_b, dlog, newk, dscaled, kern)
-    return (grad_f[None], gk[None, :n], g_gate, g_value, g_up, g_down)
+    )(gathered, gf, gk)
+    return (
+        grad_f[None],
+        jnp.transpose(grad_k, (1, 0, 2)),
+        g_gate.reshape(w_feat_gate.shape),
+        g_value.reshape(w_value.shape),
+        g_up.reshape(w_up.shape),
+        g_down.reshape(w_down.shape),
+    )
 
 
 def solution(mesh):

time: 86.2 us -> 378 us (4.39)
  Pallas kernels: 76.4 us -> 372 us
    pallas_call x1, Pallas kernels: 6.59 us -> 307 us  [shards(): pl.pallas_call(finish, out_shape=(shape((cells, channels), F32), shape((n...]
    pallas_call x1, Pallas kernels: 69.8 us -> 65.8 us  [shards(): pl.pallas_call(functools.partial(section, scale), out_shape=(shape((2, ZH...]
    unnamed x15 -> x6, local copies, waits for them, and re-layouts: 8.78 us -> 5.11 us
where the time goes in v2:
time: 378 us
  Pallas kernels  372 us (98%)
  local copies, waits for them, and re-layouts  5.11 us (1%)
    pallas_call x1, Pallas kernels, shards(): pl.pallas_call(finish, out_shape=(shape((cells, channels), F32), shape((n...  307 us
    pallas_call x1, Pallas kernels, shards(): pl.pallas_call(functools.partial(section, scale), out_shape=(shape((2, ZH...  65.8 us

profile of v2, /device:TPU:1, one launch (start us, length us, event | category | flops | bytes accessed | tf_op | source)
XLA Modules:
  0.0 378.2 jit_solution(15650328483873667485)
XLA Ops:
  0.6 65.8 %section.1 = (f32[2,2,4,4,144,128]{5,4,3,2,1,0:T(8,128)S(1)}, f32[5120,256]{1,0:T(8,128)S(1)}, f32[100,1,256]{2,1,0:T(1,128)S(1)}) custom-call(bf16[5120,256]{1,0:T(8,128)(2,1)} %bitcast.9, bf16[100,256]{1,0:T(8,128)(2,1)} %bitcast.11, bf16[100,5120]{1,0:T(8,128)(2,1)} %bitcast.10, bf16[256,256]{1,0:T(8,128)(2,1)} %wfg_in.1, bf16[256,256]{1,0:T(8,128)(2,1)} %wval_in.1, ...), custom_call_target="tpu_custom_call" | custom-call | tf_op jit(solution)/shard_map/section/pallas_call | solution.py:520
  66.5 0.0 copy-start
  66.5 2.3 copy-done
  68.8 0.0 copy-start.1
  68.8 2.2 copy-done.1
  71.0 0.0 copy-start.2
  71.0 0.6 copy-done.2
  71.6 306.6 %finish.1 = (f32[5120,256]{1,0:T(8,128)}, f32[100,1,256]{2,1,0:T(1,128)}, f32[8,4,8,256]{3,2,1,0:T(8,128)}, f32[8,4,8,256]{3,2,1,0:T(8,128)}, f32[4,64,2048]{2,1,0:T(8,128)}, /*index=5*/f32[8,4,64,256]{3,2,1,0:T(8,128)}) custom-call(f32[2,2,4,4,144,128]{5,4,3,2,1,0:T(8,128)} %copy-done.1, f32[5120,256]{1,0:T(8,128)} %copy-done, f32[100,1,256]{2,1,0:T(1,128)} %copy-done.2), custom_call_target="tpu_custom_call" | custom-call | tf_op jit(solution)/shard_map/finish/pallas_call | solution.py:568
Async XLA Ops:
  66.5 2.3 copy-start
  68.8 2.2 copy-start.1
  71.0 0.6 copy-start.2

commit v3 on v2

--- a/solution.py
+++ b/solution.py
@@ -513,7 +513,9 @@
     def hbm(v):
         return pltpu.with_memory_space_constraint(v, pltpu.HBM)
 
-    kern, cot = hbm(kern), hbm(cot)
+    def vmem_array(v):
+        return pltpu.with_memory_space_constraint(v, pltpu.VMEM)
+
     vmem = pl.BlockSpec(memory_space=pltpu.VMEM)
     copies = 128
     shape = jax.ShapeDtypeStruct
@@ -562,7 +564,7 @@
             collective_id=0, has_side_effects=True, vmem_limit_bytes=32 * 2**20
         ),
         name="section",
-    )(hbm(feat), kern, cot, hbm(w_feat_gate), hbm(w_value), hbm(w_up), hbm(w_down))
+    )(hbm(feat), hbm(kern), hbm(cot), hbm(w_feat_gate), hbm(w_value), hbm(w_up), hbm(w_down))
 
     tiles = ZH * Y
     grad_f, grad_k, g_gate, g_value, g_up, g_down = pl.pallas_call(
@@ -575,11 +577,12 @@
             shape((X, 64, w_up.shape[1]), F32),
             shape((tiles, X, 64, channels), F32),
         ),
-        in_specs=[anywhere] * 3,
+        in_specs=[vmem] * 3,
         out_specs=(anywhere,) * 6,
         scratch_shapes=[pltpu.SemaphoreType.DMA((2 + tiles * 2 * 4,))],
+        compiler_params=pltpu.CompilerParams(vmem_limit_bytes=2**20),
         name="finish",
-    )(gathered, gf, gk)
+    )(vmem_array(gathered), vmem_array(gf), vmem_array(gk))
     return (
         grad_f[None],
         jnp.transpose(grad_k, (1, 0, 2)),

time: 378 us -> 70.9 us (0.19)
  Pallas kernels: 372 us -> 70.2 us
  local copies, waits for them, and re-layouts: 5.11 us -> 0 us
    pallas_call x1, Pallas kernels: 307 us -> 4.36 us  [shards(): pl.pallas_call(finish, out_shape=(shape((cells, channels), F32), shape((n...]
    unnamed x6 -> x0, local copies, waits for them, and re-layouts: 5.11 us -> none
where the time goes in v3:
time: 70.9 us; the launch traced here: 70.8 us
  Pallas kernels  70.2 us (99%)
    pallas_call x1, Pallas kernels, shards(): pl.pallas_call(functools.partial(section, scale), out_shape=(shape((2, ZH...  65.8 us
    pallas_call x1, Pallas kernels, shards(): pl.pallas_call(finish, out_shape=(shape((cells, channels), F32), shape((n...  4.36 us

profile of v3, /device:TPU:1, one launch (start us, length us, event | category | flops | bytes accessed | tf_op | source)
XLA Modules:
  0.0 70.8 jit_solution(17721236673038421338)
XLA Ops:
  0.6 65.8 %section.1 = (f32[2,2,4,4,144,128]{5,4,3,2,1,0:T(8,128)S(1)}, f32[5120,256]{1,0:T(8,128)S(1)}, f32[100,1,256]{2,1,0:T(1,128)S(1)}) custom-call(bf16[5120,256]{1,0:T(8,128)(2,1)} %bitcast.9, bf16[100,256]{1,0:T(8,128)(2,1)} %bitcast.11, bf16[100,5120]{1,0:T(8,128)(2,1)} %bitcast.10, bf16[256,256]{1,0:T(8,128)(2,1)} %wfg_in.1, bf16[256,256]{1,0:T(8,128)(2,1)} %wval_in.1, ...), custom_call_target="tpu_custom_call" | custom-call | tf_op jit(solution)/shard_map/section/pallas_call | solution.py:522
  66.5 4.4 %finish.1 = (f32[5120,256]{1,0:T(8,128)}, f32[100,1,256]{2,1,0:T(1,128)}, f32[8,4,8,256]{3,2,1,0:T(8,128)}, f32[8,4,8,256]{3,2,1,0:T(8,128)}, f32[4,64,2048]{2,1,0:T(8,128)}, /*index=5*/f32[8,4,64,256]{3,2,1,0:T(8,128)}) custom-call(f32[2,2,4,4,144,128]{5,4,3,2,1,0:T(8,128)S(1)} %get-tuple-element.15.gathered, f32[5120,256]{1,0:T(8,128)S(1)} %get-tuple-element.16.gf, ...), custom_call_target="tpu_custom_call" | custom-call | tf_op jit(solution)/shard_map/finish/pallas_call | solution.py:570

commit v4 on v3

--- a/solution.py
+++ b/solution.py
@@ -14,9 +14,57 @@
 ROWS = 112
 PART = 56
 CHUNK = 1024
-PIECE = 32
-SMALL = 16
-BLOCK = ZL * PIECE + SMALL
+PIECE = 16
+BLOCK = 144
+PARTS = ((0, 64), (64, 80))
+SMALL = (128, 16)
+ORDER = [
+    ("l", 0, 0, 1),
+    ("l", 0, 0, 3),
+    ("r", 0, 0, 0),
+    ("l", 0, 0, 2),
+    ("m", 1, 1, 0),
+    ("l", 0, 1, 1),
+    ("l", 0, 1, 3),
+    ("r", 0, 1, 0),
+    ("l", 1, 0, 1),
+    ("l", 1, 0, 3),
+    ("l", 0, 1, 2),
+    ("r", 1, 0, 0),
+    ("r", 0, 0, 1),
+    ("l", 1, 0, 2),
+    ("r", 1, 1, 0),
+    ("r", 0, 0, 3),
+    ("c", 0, 0, 0),
+    ("r", 0, 1, 1),
+    ("r", 0, 0, 2),
+    ("r", 0, 1, 3),
+    ("c", 0, 1, 0),
+    ("l", 1, 1, 1),
+    ("l", 1, 1, 3),
+    ("r", 0, 1, 2),
+    ("c", 1, 1, 0),
+    ("c", 0, 1, 1),
+    ("c", 0, 1, 3),
+    ("l", 1, 1, 2),
+    ("r", 1, 0, 1),
+    ("r", 1, 0, 3),
+    ("r", 1, 1, 1),
+    ("c", 1, 0, 0),
+    ("c", 0, 0, 1),
+    ("r", 1, 1, 3),
+    ("c", 0, 1, 2),
+    ("r", 1, 0, 2),
+    ("c", 0, 0, 3),
+    ("r", 1, 1, 2),
+    ("c", 0, 0, 2),
+    ("c", 1, 1, 1),
+    ("c", 1, 0, 1),
+    ("c", 1, 0, 3),
+    ("c", 1, 1, 3),
+    ("c", 1, 0, 2),
+    ("c", 1, 1, 2),
+]
 NT = (((1,), (1,)), ((), ()))
 NN = (((1,), (0,)), ((), ()))
 TN = (((0,), (0,)), ((), ()))
@@ -96,14 +144,14 @@
     def __init__(self, send, recv):
         self.send, self.recv, self.n = send, recv, 0
 
-    def copy(self, src, dst, device):
+    def copy(self, src, dst, device, send=None, recv=None):
         i = self.n
         self.n += 1
         return pltpu.make_async_remote_copy(
             src_ref=src,
             dst_ref=dst,
-            send_sem=self.send.at[i],
-            recv_sem=self.recv.at[i],
+            send_sem=self.send.at[i] if send is None else send,
+            recv_sem=self.recv.at[i] if recv is None else recv,
             device_id=device,
             device_id_type=MESH,
         )
@@ -196,6 +244,7 @@
     local,
     send,
     recv,
+    shared,
 ):
     me = Place()
     sems = Sems(send, recv)
@@ -297,7 +346,24 @@
     k3, rs3 = norm(z)
     newk = k3.astype(BF16)[:n]
 
+    def slice_of(k, ref):
+        first, size = PARTS[k]
+        return ref.at[..., pl.ds(first, size), :]
+
+    def spread(first, size, v):
+        for h in range(2):
+            for i in range(X):
+                terms[h, i, first : first + size, :] = v(i)[:, h * 128 : (h + 1) * 128]
+
+    def to_other_core(k):
+        cp = sems.copy(slice_of(k, terms.at[1 - c]), slice_of(k, r0), me.at(dc=1))
+        cp.start()
+        return cp
+
     dz = norm_back(sum_d.result(), k3, rs3)
+    down_term = outer3(hid[me.tile], dz)
+    spread(0, 64, lambda i: down_term[i * 64 : (i + 1) * 64])
+    c0 = [to_other_core(0)]
     dzs = stack(dz)
     dk1 = dz
     for j in range(ff):
@@ -307,24 +373,35 @@
     du = norm_back(dk1, k1, rs1)
     dgate = du * value * (gate * (1.0 - gate))
     dvalue = du * gate
+    up_term = outer3(k1, dhid[me.tile])
+    spread(64, 64, lambda i: up_term[i * 64 : (i + 1) * 64])
+    tmp[0] = outer3(pooled, dgate)
+    tmp[1] = outer3(pooled, dvalue)
+
+    def own(i):
+        return pl.ds(pl.multiple_of(me.tile * 32 + i * 8, 8), 8)
+
+    spread(128, 8, lambda i: tmp[0, own(i), :])
+    spread(136, 8, lambda i: tmp[1, own(i), :])
+    c0.append(to_other_core(1))
+
+    def across_x(k):
+        c0[k].wait_recv()
+        first, size = PARTS[k]
+        rows = slice(first, first + size)
+        mine[:, rows, :] = terms[c, :, rows, :] + r0[:, rows, :]
+        cps = [
+            sems.copy(slice_of(k, mine.at[lax.rem(x + d, X)]), slice_of(k, r1.at[d - 1]), me.at(dx=d))
+            for d in (1, 3, 2)
+        ]
+        for cp in cps:
+            cp.start()
+        return cps
+
+    c1 = [across_x(0)]
     dpooled = dot2(stack(dgate), wfg[...], NT) + dot2(stack(dvalue), wval[...], NT)
     dscaled = (dpooled * scale).astype(BF16)
     acc[...] = du
-
-    up_term = outer3(k1, dhid[me.tile])
-    down_term = outer3(hid[me.tile], dz)
-    tmp[0] = outer3(pooled, dgate)
-    tmp[1] = outer3(pooled, dvalue)
-    for h in range(2):
-        lanes = slice(h * 128, (h + 1) * 128)
-        for i in range(X):
-            own = pl.ds(pl.multiple_of(me.tile * 32 + i * 8, 8), 8)
-            terms[h, i, :64, :] = up_term[i * 64 : (i + 1) * 64, lanes]
-            terms[h, i, 64:128, :] = down_term[i * 64 : (i + 1) * 64, lanes]
-            terms[h, i, 128:136, :] = tmp[0, own, lanes]
-            terms[h, i, 136:, :] = tmp[1, own, lanes]
-    c0 = sems.copy(terms.at[1 - c], r0, me.at(dc=1))
-    c0.start()
 
     ds = dscaled[:n]
 
@@ -344,142 +421,141 @@
             term(cot[:, part(i)], newk) + term(prob_b[:, part(i)], ds) + term(dlog[:, part(i)], kern)
         )
 
-    macc = lax.fori_loop(0, 2, mask, jnp.zeros((n, 256), F32))
-    c0.wait_recv()
-    mine[...] = terms[c] + r0[...]
-    c1 = [sems.copy(mine.at[lax.rem(x + d, X)], r1.at[d - 1], me.at(dx=d)) for d in (1, 3, 2)]
-    for cp in c1:
+    def piece(k, i):
+        return pl.ds(pl.multiple_of(PARTS[k][0] + i * PIECE, PIECE), PIECE)
+
+    tail = pl.ds(*SMALL)
+
+    def across_z(k):
+        for cp in c1[k]:
+            cp.wait_recv()
+        rows = slice(PARTS[k][0], sum(PARTS[k]))
+        half[rows, :] = (mine[x, rows, :] + r1[0, rows, :]) + (r1[1, rows, :] + r1[2, rows, :])
+        cps = [
+            sems.copy(half.at[piece(k, lax.rem(zl + d, ZL)), :], r2.at[d - 1, k], me.at(dzl=d))
+            for d in (1, 3, 2)
+        ]
+        if k == 1:
+            small[zl] = half[tail, :]
+            cps += [sems.copy(half.at[tail, :], small.at[zl], me.at(dzl=d)) for d in (1, 3, 2)]
+        for cp in cps:
+            cp.start()
+        return cps
+
+    def along_z(k):
+        for cp in c2[k]:
+            cp.wait_recv()
+        gathered[c, zh, y, x, piece(k, zl), :] = (half[piece(k, zl), :] + r2[0, k]) + (r2[1, k] + r2[2, k])
+        here = gathered.at[c, zh, y, x, piece(k, zl), :]
+        near = [sems.copy(here, here, me.at(dzl=d)) for d in (1, 3, 2)]
+        far = [sems.copy(here, here, me.at(dzl=d, dzh=1)) for d in (0, 1, 3, 2)]
+        if k == 1:
+            gathered[c, zh, y, x, tail, :] = (small[0] + small[1]) + (small[2] + small[3])
+            here = gathered.at[c, zh, y, x, tail, :]
+            far.append(sems.copy(here, here, me.at(dzh=1)))
+        for cp in near + far:
+            cp.start()
+        return near, far
+
+    mids, lasts, relays = {}, {}, {}
+
+    def axes(q):
+        my = lax.rem(zh + q, ZH)
+        return 1 - my, my
+
+    def block(q, m, l):
+        mx, my = axes(q)
+        bx = lax.rem(x + mx * m + my * l, X)
+        by = lax.rem(y + my * m + mx * l, Y)
+        return gathered.at[c, lax.rem(zh + q, ZH), by, bx]
+
+    def send_to(b, device):
+        cp = sems.copy(b, b, device, send=shared.at[0])
         cp.start()
-    macc = lax.fori_loop(2, chunks, mask, macc)
+        return cp
+
+    def to_twin(b):
+        sems.copy(b, b, me.at(dc=1), send=shared.at[1], recv=shared.at[2]).start()
+
+    def along_mid(q, d):
+        mx, my = axes(q)
+        return me.at(dx=mx * d, dy=my * d)
+
+    def along_last(q, d):
+        mx, my = axes(q)
+        return me.at(dx=my * d, dy=mx * d)
+
+    def have(k, *spot):
+        to_twin(slice_of(k, block(*spot)))
+
+    def open_mid(k, q):
+        for cp in zs[k][q]:
+            cp.wait_recv()
+        b = slice_of(k, block(q, 0, 0))
+        for d in (1, 3, 2):
+            mids[k, q, d] = send_to(b, along_mid(q, d))
+        open_last(k, q, 0)
+
+    def open_last(k, q, m):
+        if m:
+            mids[k, q, m].wait_recv()
+        b = slice_of(k, block(q, (4 - m) % 4, 0))
+        lasts[k, q, m] = {d: send_to(b, along_last(q, d)) for d in (1, 3)}
+        have(k, q, (4 - m) % 4, 0)
+
+    def relay(k, q, m):
+        relays[k, q, m] = []
+        size = PARTS[k][1] // 2
+        for d, first in ((1, PARTS[k][0]), (3, PARTS[k][0] + size)):
+            lasts[k, q, m][d].wait_recv()
+            b = block(q, (4 - m) % 4, 4 - d).at[pl.ds(first, size), :]
+            relays[k, q, m].append(send_to(b, along_last(q, d)))
+            have(k, q, (4 - m) % 4, 4 - d)
+
+    def close(k, q, m):
+        for cp in relays[k, q, m]:
+            cp.wait_recv()
+        have(k, q, (4 - m) % 4, 2)
+
+    c1.append(across_x(1))
+    macc = lax.fori_loop(0, 3, mask, jnp.zeros((n, 256), F32))
+    c2 = [across_z(0)]
+    macc = lax.fori_loop(3, chunks, mask, macc)
     acc2[...] = jnp.zeros_like(acc2)
     acc2[:n, :] = macc
     place(sums.at[2], acc2[...])
     sum_m.scatter()
-    for cp in c1:
-        cp.wait_recv()
-    half[...] = (mine[x] + r1[0]) + (r1[1] + r1[2])
-
-    def piece(i):
-        return pl.ds(pl.multiple_of(i * PIECE, PIECE), PIECE)
-
-    tail = pl.ds(ZL * PIECE, SMALL)
-    small[zl] = half[ZL * PIECE :, :]
-    c2 = []
-    for d in (1, 3, 2):
-        c2.append(sems.copy(half.at[piece(lax.rem(zl + d, ZL)), :], r2.at[d - 1], me.at(dzl=d)))
-        c2.append(sems.copy(half.at[tail, :], small.at[zl], me.at(dzl=d)))
-    for cp in c2:
-        cp.start()
+    c2.append(across_z(1))
+    features(0)
+    zs = [along_z(0)]
     sum_m.exchange()
-    features(0)
-    for cp in c2:
-        cp.wait_recv()
-
-    gathered[c, zh, y, x, piece(zl), :] = (half[piece(zl), :] + r2[0]) + (r2[1] + r2[2])
-    gathered[c, zh, y, x, tail, :] = (small[0] + small[1]) + (small[2] + small[3])
-    here = gathered.at[c, zh, y, x, piece(zl), :]
-    here_tail = gathered.at[c, zh, y, x, tail, :]
-    far = [sems.copy(here, here, me.at(dzl=d, dzh=1)) for d in (0, 1, 3, 2)]
-    far.append(sems.copy(here_tail, here_tail, me.at(dzh=1)))
-    near = [sems.copy(here, here, me.at(dzl=d)) for d in (1, 3, 2)]
-    for cp in near + far:
-        cp.start()
+    features(1)
+    zs.append(along_z(1))
+    features(2)
+    open_mid(0, 0)
+    features(3)
+    open_mid(0, 1)
+    open_mid(1, 0)
     sum_m.gather()
-    features(1)
-
-    mx, my = 1 - c, c
-
-    def block(q, m, l):
-        bx = lax.rem(x + mx * m + my * l, X)
-        by = lax.rem(y + my * m + mx * l, Y)
-        return gathered.at[c, lax.rem(zh + q, ZH), by, bx]
-
-    started = []
-    twin = []
-
-    def send_to(b, device):
-        cp = sems.copy(b, b, device)
-        cp.start()
-        started.append(cp)
-        return cp
-
-    def along_mid(d):
-        return me.at(dx=mx * d, dy=my * d)
-
-    def along_last(d):
-        return me.at(dx=my * d, dy=mx * d)
-
-    def to_twin(b):
-        twin.append(send_to(b, me.at(dc=1)))
-
-    mids, lasts, halves = {}, {}, {}
-
-    def open_mid(q):
-        b = block(q, 0, 0)
-        for d in (1, 3, 2):
-            mids[q, d] = send_to(b, along_mid(d))
-
-    def open_last(q, m):
-        if m:
-            mids[q, m].wait_recv()
-        b = block(q, (4 - m) % 4, 0)
-        lasts[q, m] = [send_to(b, along_last(d)) for d in (1, 3)]
-        to_twin(b)
-
-    def relay(q, m):
-        halves[q, m] = []
-        for d, first, cp in zip((1, 3), (0, BLOCK // 2), lasts[q, m]):
-            cp.wait_recv()
-            b = block(q, (4 - m) % 4, 4 - d)
-            halves[q, m].append(send_to(b.at[pl.ds(first, BLOCK // 2), :], along_last(d)))
-            to_twin(b)
-
-    def close(q, m):
-        for cp in halves[q, m]:
-            cp.wait_recv()
-        to_twin(block(q, (4 - m) % 4, 2))
-
-    for cp in near:
-        cp.wait_recv()
-    open_mid(0)
-    open_last(0, 0)
-    features(2)
-    for cp in far:
-        cp.wait_recv()
-    open_mid(1)
-    open_last(1, 0)
-    features(3)
-    relay(0, 0)
-    open_last(0, 1)
-    open_last(0, 3)
-    relay(1, 0)
-    open_last(1, 1)
-    open_last(1, 3)
-    open_last(0, 2)
-    open_last(1, 2)
-    close(0, 0)
     features(4)
-    relay(0, 1)
-    relay(0, 3)
-    close(1, 0)
-    relay(1, 1)
-    relay(1, 3)
+    rest = {"l": open_last, "r": relay, "c": close}
+    for step, k, q, m in ORDER:
+        if step == "m":
+            open_mid(k, q)
+        else:
+            rest[step](k, q, m)
     gk_out[:, 0, :] = (sum_m.result() + acc[...])[:n]
-    close(0, 1)
-    close(0, 3)
-    relay(0, 2)
-    relay(1, 2)
-    close(1, 1)
-    close(1, 3)
-    close(0, 2)
-    close(1, 2)
-    for cp in twin:
-        cp.wait_recv()
+    half_of_all = gathered.at[0]
+    for i in (2, 1):
+        pltpu.make_async_copy(half_of_all, half_of_all, shared.at[i]).wait()
+    for sent in (gathered.at[0, 0], gathered.at[0, 1, pl.ds(0, 3)], gathered.at[1, 0, 0, pl.ds(0, 2)]):
+        pltpu.make_async_copy(sent, sent, shared.at[0]).wait()
 
     for s in (sum_p, sum_d, sum_m):
         s.close()
-    for cp in [c0] + c1 + c2 + near + far + started:
-        cp.wait_send()
+    for k in range(2):
+        for cp in [c0[k]] + c1[k] + c2[k] + zs[k][0] + zs[k][1]:
+            cp.wait_send()
 
 
 def finish(gathered, gf, gk, grad_f, grad_k, g_gate, g_value, g_up, g_down, sem):
@@ -489,8 +565,8 @@
         for t in range(ZH * Y):
             src = gathered.at[h, t // Y, t % Y]
             pairs += [
-                (src.at[:, 0:64, :], g_up.at[:, :, pl.ds(t * 256 + h * 128, 128)]),
-                (src.at[:, 64:128, :], g_down.at[t, :, :, lanes]),
+                (src.at[:, 0:64, :], g_down.at[t, :, :, lanes]),
+                (src.at[:, 64:128, :], g_up.at[:, :, pl.ds(t * 256 + h * 128, 128)]),
                 (src.at[:, 128:136, :], g_gate.at[t, :, :, lanes]),
                 (src.at[:, 136:144, :], g_value.at[t, :, :, lanes]),
             ]
@@ -517,7 +593,7 @@
         return pltpu.with_memory_space_constraint(v, pltpu.VMEM)
 
     vmem = pl.BlockSpec(memory_space=pltpu.VMEM)
-    copies = 128
+    copies = 200
     shape = jax.ShapeDtypeStruct
     gathered, gf, gk = pl.pallas_call(
         functools.partial(section, scale),
@@ -554,11 +630,12 @@
             pltpu.VMEM((X, BLOCK, 128), F32),
             pltpu.VMEM((3, BLOCK, 128), F32),
             pltpu.VMEM((BLOCK, 128), F32),
-            pltpu.VMEM((3, PIECE, 128), F32),
-            pltpu.VMEM((ZL, SMALL, 128), F32),
+            pltpu.VMEM((3, 2, PIECE, 128), F32),
+            pltpu.VMEM((ZL, SMALL[1], 128), F32),
             pltpu.SemaphoreType.DMA((2 * chunks + 5,)),
             pltpu.SemaphoreType.DMA((copies,)),
             pltpu.SemaphoreType.DMA((copies,)),
+            pltpu.SemaphoreType.DMA((3,)),
         ],
         compiler_params=pltpu.CompilerParams(
             collective_id=0, has_side_effects=True, vmem_limit_bytes=32 * 2**20

time: 70.9 us -> 68.8 us (0.970)
  Pallas kernels: 70.2 us -> 68 us
    pallas_call x1, Pallas kernels: 65.8 us -> 63.7 us  [shards(): pl.pallas_call(functools.partial(section, scale), out_shape=(shape((2, ZH...]
where the time goes in v4:
time: 68.8 us; the launch traced here: 68.7 us
  Pallas kernels  68 us (99%)
    pallas_call x1, Pallas kernels, shards(): pl.pallas_call(functools.partial(section, scale), out_shape=(shape((2, ZH...  63.7 us
    pallas_call x1, Pallas kernels, shards(): pl.pallas_call(finish, out_shape=(shape((cells, channels), F32), shape((n...  4.36 us

profile of v4, /device:TPU:1, one launch (start us, length us, event | category | flops | bytes accessed | tf_op | source)
XLA Modules:
  0.0 68.7 jit_solution(7298578389729300979)
XLA Ops:
  0.6 63.7 %section.1 = (f32[2,2,4,4,144,128]{5,4,3,2,1,0:T(8,128)S(1)}, f32[5120,256]{1,0:T(8,128)S(1)}, f32[100,1,256]{2,1,0:T(1,128)S(1)}) custom-call(bf16[5120,256]{1,0:T(8,128)(2,1)} %bitcast.9, bf16[100,256]{1,0:T(8,128)(2,1)} %bitcast.11, bf16[100,5120]{1,0:T(8,128)(2,1)} %bitcast.10, bf16[256,256]{1,0:T(8,128)(2,1)} %wfg_in.1, bf16[256,256]{1,0:T(8,128)(2,1)} %wval_in.1, ...), custom_call_target="tpu_custom_call" | custom-call | tf_op jit(solution)/shard_map/section/pallas_call | solution.py:598
  64.3 4.4 %finish.1 = (f32[5120,256]{1,0:T(8,128)}, f32[100,1,256]{2,1,0:T(1,128)}, f32[8,4,8,256]{3,2,1,0:T(8,128)}, f32[8,4,8,256]{3,2,1,0:T(8,128)}, f32[4,64,2048]{2,1,0:T(8,128)}, /*index=5*/f32[8,4,64,256]{3,2,1,0:T(8,128)}) custom-call(f32[2,2,4,4,144,128]{5,4,3,2,1,0:T(8,128)S(1)} %get-tuple-element.15.gathered, f32[5120,256]{1,0:T(8,128)S(1)} %get-tuple-element.16.gf, ...), custom_call_target="tpu_custom_call" | custom-call | tf_op jit(solution)/shard_map/finish/pallas_call | solution.py:647

commit v5 on v4

--- a/solution.py
+++ b/solution.py
@@ -370,21 +370,6 @@
         da = dot2(dzs, wdown[j * 256 : (j + 1) * 256, :], NT) * slope[j]
         dhid[j] = da
         dk1 = dk1 + dot2(stack(da), wup[:, j * 256 : (j + 1) * 256], NT)
-    du = norm_back(dk1, k1, rs1)
-    dgate = du * value * (gate * (1.0 - gate))
-    dvalue = du * gate
-    up_term = outer3(k1, dhid[me.tile])
-    spread(64, 64, lambda i: up_term[i * 64 : (i + 1) * 64])
-    tmp[0] = outer3(pooled, dgate)
-    tmp[1] = outer3(pooled, dvalue)
-
-    def own(i):
-        return pl.ds(pl.multiple_of(me.tile * 32 + i * 8, 8), 8)
-
-    spread(128, 8, lambda i: tmp[0, own(i), :])
-    spread(136, 8, lambda i: tmp[1, own(i), :])
-    c0.append(to_other_core(1))
-
     def across_x(k):
         c0[k].wait_recv()
         first, size = PARTS[k]
@@ -399,6 +384,21 @@
         return cps
 
     c1 = [across_x(0)]
+    du = norm_back(dk1, k1, rs1)
+    dgate = du * value * (gate * (1.0 - gate))
+    dvalue = du * gate
+    up_term = outer3(k1, dhid[me.tile])
+    spread(64, 64, lambda i: up_term[i * 64 : (i + 1) * 64])
+    tmp[0] = outer3(pooled, dgate)
+    tmp[1] = outer3(pooled, dvalue)
+
+    def own(i):
+        return pl.ds(pl.multiple_of(me.tile * 32 + i * 8, 8), 8)
+
+    spread(128, 8, lambda i: tmp[0, own(i), :])
+    spread(136, 8, lambda i: tmp[1, own(i), :])
+    c0.append(to_other_core(1))
+
     dpooled = dot2(stack(dgate), wfg[...], NT) + dot2(stack(dvalue), wval[...], NT)
     dscaled = (dpooled * scale).astype(BF16)
     acc[...] = du
@@ -518,25 +518,26 @@
         have(k, q, (4 - m) % 4, 2)
 
     c1.append(across_x(1))
-    macc = lax.fori_loop(0, 3, mask, jnp.zeros((n, 256), F32))
+    macc = lax.fori_loop(0, 2, mask, jnp.zeros((n, 256), F32))
     c2 = [across_z(0)]
-    macc = lax.fori_loop(3, chunks, mask, macc)
+    macc = lax.fori_loop(2, 4, mask, macc)
+    c2.append(across_z(1))
+    macc = lax.fori_loop(4, chunks, mask, macc)
+    zs = [along_z(0)]
     acc2[...] = jnp.zeros_like(acc2)
     acc2[:n, :] = macc
     place(sums.at[2], acc2[...])
     sum_m.scatter()
-    c2.append(across_z(1))
     features(0)
-    zs = [along_z(0)]
+    zs.append(along_z(1))
     sum_m.exchange()
     features(1)
-    zs.append(along_z(1))
+    open_mid(0, 0)
     features(2)
-    open_mid(0, 0)
-    features(3)
     open_mid(0, 1)
     open_mid(1, 0)
     sum_m.gather()
+    features(3)
     features(4)
     rest = {"l": open_last, "r": relay, "c": close}
     for step, k, q, m in ORDER:

time: 68.8 us -> 70 us (1.017)
  Pallas kernels: 68 us -> 69.3 us
    pallas_call x1, Pallas kernels: 63.7 us -> 65 us  [shards(): pl.pallas_call(functools.partial(section, scale), out_shape=(shape((2, ZH...]
where the time goes in v5:
time: 70 us
  Pallas kernels  69.3 us (99%)
    pallas_call x1, Pallas kernels, shards(): pl.pallas_call(functools.partial(section, scale), out_shape=(shape((2, ZH...  65 us
    pallas_call x1, Pallas kernels, shards(): pl.pallas_call(finish, out_shape=(shape((cells, channels), F32), shape((n...  4.36 us

profile of v5, /device:TPU:1, one launch (start us, length us, event | category | flops | bytes accessed | tf_op | source)
XLA Modules:
  0.0 70.0 jit_solution(5829271262606086444)
XLA Ops:
  0.6 65.0 %section.1 = (f32[2,2,4,4,144,128]{5,4,3,2,1,0:T(8,128)S(1)}, f32[5120,256]{1,0:T(8,128)S(1)}, f32[100,1,256]{2,1,0:T(1,128)S(1)}) custom-call(bf16[5120,256]{1,0:T(8,128)(2,1)} %bitcast.9, bf16[100,256]{1,0:T(8,128)(2,1)} %bitcast.11, bf16[100,5120]{1,0:T(8,128)(2,1)} %bitcast.10, bf16[256,256]{1,0:T(8,128)(2,1)} %wfg_in.1, bf16[256,256]{1,0:T(8,128)(2,1)} %wval_in.1, ...), custom_call_target="tpu_custom_call" | custom-call | tf_op jit(solution)/shard_map/section/pallas_call | solution.py:599
  65.6 4.4 %finish.1 = (f32[5120,256]{1,0:T(8,128)}, f32[100,1,256]{2,1,0:T(1,128)}, f32[8,4,8,256]{3,2,1,0:T(8,128)}, f32[8,4,8,256]{3,2,1,0:T(8,128)}, f32[4,64,2048]{2,1,0:T(8,128)}, /*index=5*/f32[8,4,64,256]{3,2,1,0:T(8,128)}) custom-call(f32[2,2,4,4,144,128]{5,4,3,2,1,0:T(8,128)S(1)} %get-tuple-element.15.gathered, f32[5120,256]{1,0:T(8,128)S(1)} %get-tuple-element.16.gf, ...), custom_call_target="tpu_custom_call" | custom-call | tf_op jit(solution)/shard_map/finish/pallas_call | solution.py:648
